TPU v7x, 32 devices: a whole 2x2x4 slice. The times are simulated.
32 devices in a mesh: dp: 2 (over x), shard: 16 (over z, y, core).
Axes of the slice: x: 2, y: 2, z: 4, core: 2. Of those that a mesh axis runs over, the one named last changes fastest.
Arguments:
- trajectories: float32 [2048, 32, 23], P(('dp', 'shard')), may hold values from -6 to 6
- noise: float32 [2048, 32, 23], P(('dp', 'shard')), may hold values from -6 to 6
- timesteps: int32 [2048], P(('dp', 'shard')), may hold values from 0 to 19
- valid: int32 [2048, 32], P(('dp', 'shard')), may hold values from 0 to 1, as said below
- owners: int32 [67], replicated, may hold values from 0 to 79, as said below
- mat_weight: float32 [67, 128, 256], P(None, 'shard')
- mat_ema: float32 [67, 128, 256], P(None, 'shard')
- soap_first: float32 [80, 128, 256], P('shard'), may hold values from -5.340576e-05 to 5.340576e-05
- soap_second: float32 [80, 128, 256], P('shard'), may hold values from 5.834243e-11 to 2.378576e-10
- left_stat: float32 [80, 128, 128], P('shard'), as said below
- right_stat: float32 [80, 256, 256], P('shard'), as said below
- left_basis: float32 [80, 128, 128], P('shard'), as said below
- right_basis: float32 [80, 256, 256], P('shard'), as said below
- vec_weight: float32 [128, 256], P('shard')
- vec_first: float32 [128, 256], P('shard'), may hold values from -0.00048828125 to 0.00048828125
- vec_second: float32 [128, 256], P('shard'), may hold values from 5.3854547e-09 to 2.1093031e-08
- vec_ema: float32 [128, 256], P('shard')
Outputs:
- loss_sum: float32 [], replicated
- count: float32 [], replicated
- grad_norm: float32 [], replicated
- new_mat: float32 [67, 128, 256], P(None, 'shard')
- new_mat_ema: float32 [67, 128, 256], P(None, 'shard')
- new_first: float32 [80, 128, 256], P('shard')
- new_second: float32 [80, 128, 256], P('shard')
- new_left_stat: float32 [80, 128, 128], P('shard')
- new_right_stat: float32 [80, 256, 256], P('shard')
- new_left_basis: float32 [80, 128, 128], P('shard')
- new_right_basis: float32 [80, 256, 256], P('shard')
- new_vec: float32 [128, 256], P('shard')
- new_vec_first: float32 [128, 256], P('shard')
- new_vec_second: float32 [128, 256], P('shard')
- new_vec_ema: float32 [128, 256], P('shard')
Inputs may be any that keep to these rules, and one draw needn't show every extreme that they name: `valid`: the first frame of every trajectory counts. `owners`: distinct slots; the last slot always holds a block. `left_stat`: symmetric positive definite. `right_stat`: symmetric positive definite. `left_basis`: Nonsingular. `right_basis`: Nonsingular.
All inputs are finite; a program needn't handle non-finite values.
Results may differ from a plain program's by a relative error of at most 0.01.
Values may be sent and summed in bfloat16 or wider, within the bound.
A program may use at most 192 MiB of HBM per device.

v0:
```python
import math

import jax
import jax.numpy as jnp
from jax import lax
from jax.sharding import PartitionSpec as P

WIDTH = 256
KERNEL = 5
GROUPS = 8
TDIM = 128
FEAT = 23
BLOCKS = 3
DSTEPS = 20
STEP = 10
OWNED = 6
UNITS = 67
VROWS = 128


HIGH = lax.Precision.HIGHEST
BETA_ONE = 0.9
BETA_TWO = 0.95
ADAM_EPS = 1e-08
LEARN = 0.05
TABLE_LEARN = 0.25
DECAY = 0.01
CLIP = 0.05
EMA_RATE = 0.8
NORM_EPS = 1e-05


def vec_base():
    return 2 * FEAT


def block_vectors(table, block):
    conv_row = vec_base() + 3 + 2 * block
    gain_row = conv_row + OWNED
    shift_row = conv_row + 2 * OWNED
    return (
        table[conv_row],
        table[gain_row],
        table[shift_row],
        table[conv_row + 1],
        table[gain_row + 1],
        table[shift_row + 1],
    )


def bias_row(block):
    return vec_base() + 3 + 3 * OWNED + block


def conv_matrix(mats, index):
    taps = 2 * KERNEL
    return mats[index * taps : (index + 1) * taps].reshape(KERNEL * WIDTH, WIDTH)


def lin_matrix(mats, block):
    start = 2 * KERNEL * OWNED + 2 * block
    return mats[start : start + 2].reshape(WIDTH, WIDTH)


def mish_act(v):
    return v * jnp.tanh(jax.nn.softplus(v))


def group_norm(v, gain, shift):
    grouped = v.reshape(v.shape[0], v.shape[1], GROUPS, v.shape[2] // GROUPS)
    centre = jnp.mean(grouped, axis=(1, 3), keepdims=True)
    spread = jnp.mean((grouped - centre) ** 2, axis=(1, 3), keepdims=True)
    normed = ((grouped - centre) * lax.rsqrt(spread + NORM_EPS)).reshape(v.shape)
    return normed * gain + shift


def unfold_taps(v):
    margin = KERNEL // 2
    padded = jnp.pad(v, ((0, 0), (margin, margin), (0, 0)))
    frames = v.shape[1]
    return jnp.concatenate([padded[:, index : index + frames] for index in range(KERNEL)], axis=-1)


def fold_taps(grads):
    margin = KERNEL // 2
    frames = grads.shape[1]
    width = grads.shape[2] // KERNEL
    padded = jnp.pad(grads, ((0, 0), (margin, margin), (0, 0)))
    total = jnp.zeros((grads.shape[0], frames, width), jnp.float32)
    for index in range(KERNEL):
        begin = 2 * margin - index
        total = total + padded[:, begin : begin + frames, index * width : (index + 1) * width]
    return total


def noise_level(steps):
    offset = 0.008
    ratio = (steps.astype(jnp.float32) + 1.0) / DSTEPS
    upper = jnp.cos((ratio + offset) / (1.0 + offset) * math.pi / 2) ** 2
    return upper / math.cos(offset / (1.0 + offset) * math.pi / 2) ** 2


def time_embed(steps):
    halfway = TDIM // 2
    freqs = jnp.exp(-math.log(10000.0) * jnp.arange(halfway, dtype=jnp.float32) / (halfway - 1))
    angles = steps.astype(jnp.float32)[:, None] * freqs[None, :]
    return jnp.concatenate([jnp.sin(angles), jnp.cos(angles)], axis=-1)


def conv_mat(taps, weight):
    return jnp.einsum("bfk,kw->bfw", taps, weight, preferred_element_type=jnp.float32)


def grad_mat(taps, grads):
    return jnp.einsum("bfk,bfw->kw", taps, grads, preferred_element_type=jnp.float32)


def back_mat(grads, weight):
    return jnp.einsum("bfw,kw->bfk", grads, weight, preferred_element_type=jnp.float32)


def piece_first(pre_a, conv_bias, gain, shift, t_bias):
    return mish_act(group_norm(pre_a + conv_bias, gain, shift)) + t_bias[:, None, :]


def piece_second(pre_b, conv_bias, gain, shift, h_in):
    return h_in + mish_act(group_norm(pre_b + conv_bias, gain, shift))


def block_forward(h_in, w_first, w_second, vectors, t_bias):
    middle = piece_first(
        conv_mat(unfold_taps(h_in.astype(jnp.bfloat16)), w_first),
        vectors[0],
        vectors[1],
        vectors[2],
        t_bias,
    )
    return piece_second(
        conv_mat(unfold_taps(middle.astype(jnp.bfloat16)), w_second),
        vectors[3],
        vectors[4],
        vectors[5],
        h_in,
    )


def block_backward(h_in, d_out, w_first, w_second, vectors, t_bias):
    taps_a = unfold_taps(h_in.astype(jnp.bfloat16))
    middle, pull_first = jax.vjp(
        piece_first, conv_mat(taps_a, w_first), vectors[0], vectors[1], vectors[2], t_bias
    )
    taps_b = unfold_taps(middle.astype(jnp.bfloat16))
    _, pull_second = jax.vjp(
        piece_second, conv_mat(taps_b, w_second), vectors[3], vectors[4], vectors[5], h_in
    )
    d_pre_b, g_cb, g_gb, g_sb, d_resid = pull_second(d_out)
    d_pre_b = d_pre_b.astype(jnp.bfloat16)
    grad_second = grad_mat(taps_b, d_pre_b)
    d_middle = fold_taps(back_mat(d_pre_b, w_second))
    d_pre_a, g_ca, g_ga, g_sa, d_tbias = pull_first(d_middle)
    d_pre_a = d_pre_a.astype(jnp.bfloat16)
    grad_first = grad_mat(taps_a, d_pre_a)
    d_in = d_resid + fold_taps(back_mat(d_pre_a, w_first))
    return (d_in, grad_first, grad_second, (g_ca, g_ga, g_sa, g_cb, g_gb, g_sb), d_tbias)


def orthonormal(matrix):
    gram = jnp.dot(matrix.T, matrix, precision=HIGH)
    lower = jnp.linalg.cholesky(gram)
    return jax.scipy.linalg.solve_triangular(lower, matrix.T, lower=True).T


def rotate_in(matrix, left, right):
    return jnp.dot(jnp.dot(left.T, matrix, precision=HIGH), right, precision=HIGH)


def rotate_out(matrix, left, right):
    return jnp.dot(jnp.dot(left, matrix, precision=HIGH), right.T, precision=HIGH)


def soap_slot(grad, first, second, left_stat, right_stat, left_basis, right_basis):
    first_new = BETA_ONE * first + (1.0 - BETA_ONE) * grad
    turned = rotate_in(grad, left_basis, right_basis)
    second_new = BETA_TWO * second + (1.0 - BETA_TWO) * turned * turned
    moment = rotate_in(first_new, left_basis, right_basis)
    normed = (
        moment / (1.0 - BETA_ONE**STEP) / (jnp.sqrt(second_new / (1.0 - BETA_TWO**STEP)) + ADAM_EPS)
    )
    update = rotate_out(normed, left_basis, right_basis)
    left_new = BETA_TWO * left_stat + (1.0 - BETA_TWO) * jnp.dot(grad, grad.T, precision=HIGH)
    right_new = BETA_TWO * right_stat + (1.0 - BETA_TWO) * jnp.dot(grad.T, grad, precision=HIGH)
    left_next = orthonormal(jnp.dot(left_new, left_basis, precision=HIGH))
    right_next = orthonormal(jnp.dot(right_new, right_basis, precision=HIGH))
    return (update, first_new, second_new, left_new, right_new, left_next, right_next)


def body(
    trajectories,
    noise,
    timesteps,
    valid,
    owners,
    mat_weight,
    mat_ema,
    soap_first,
    soap_second,
    left_stat,
    right_stat,
    left_basis,
    right_basis,
    vec_weight,
    vec_first,
    vec_second,
    vec_ema,
):
    base = vec_base()
    half_rows = WIDTH // 2
    mask = valid.astype(jnp.float32)
    count_local = FEAT * jnp.sum(mask)
    count_total = lax.psum(count_local, ("dp", "shard"))
    mat_low = lax.all_gather(mat_weight.astype(jnp.bfloat16), "shard", axis=1, tiled=True)
    table = lax.all_gather(vec_weight, "shard", axis=0, tiled=True)
    table_low = table.astype(jnp.bfloat16)
    level = noise_level(timesteps)[:, None, None]
    noisy = (jnp.sqrt(level) * trajectories + jnp.sqrt(1.0 - level) * noise).astype(jnp.bfloat16)
    emb = time_embed(timesteps).astype(jnp.bfloat16)
    pre_time = jnp.dot(emb, mat_low[UNITS - 1], preferred_element_type=jnp.float32)
    time_act, pull_time = jax.vjp(lambda pre, bias: mish_act(pre + bias), pre_time, table[base + 1])
    temb = time_act.astype(jnp.bfloat16)
    t_biases = [
        jnp.dot(temb, lin_matrix(mat_low, block), preferred_element_type=jnp.float32)
        + table[bias_row(block)]
        for block in range(BLOCKS)
    ]
    hidden = conv_mat(noisy, table_low[:FEAT]) + table[base]
    stored = []
    skip = hidden
    for block in range(BLOCKS):
        if block == BLOCKS - 1:
            hidden = hidden + skip
        stored.append(hidden)
        hidden = block_forward(
            hidden,
            conv_matrix(mat_low, 2 * block),
            conv_matrix(mat_low, 2 * block + 1),
            block_vectors(table, block),
            t_biases[block],
        )
        if block == 0:
            skip = hidden
    top = hidden.astype(jnp.bfloat16)
    head_mat = table_low[FEAT : 2 * FEAT]
    pred = (
        jnp.einsum("bfw,cw->bfc", top, head_mat, preferred_element_type=jnp.float32)
        + table[base + 2, :FEAT]
    )
    error = pred - noise
    loss_local = jnp.sum(mask[:, :, None] * error * error)
    d_pred = 2.0 * mask[:, :, None] * error
    g_head_bias = jnp.sum(d_pred, axis=(0, 1))
    d_pred_low = d_pred.astype(jnp.bfloat16)
    g_head = jnp.einsum("bfc,bfw->cw", d_pred_low, top, preferred_element_type=jnp.float32)
    d_hidden = jnp.einsum("bfc,cw->bfw", d_pred_low, head_mat, preferred_element_type=jnp.float32)
    mat_back = lax.all_gather(mat_weight.astype(jnp.bfloat16), "shard", axis=1, tiled=True)
    conv_grads = [None] * OWNED
    vec_grads = [None] * BLOCKS
    tbias_grads = [None] * BLOCKS
    tmat_grads = [None] * BLOCKS
    d_temb = jnp.zeros(time_act.shape, jnp.float32)
    d_skip = d_hidden
    for block in reversed(range(BLOCKS)):
        d_in, grad_first, grad_second, g_vecs, d_tbias = block_backward(
            stored[block],
            d_hidden,
            conv_matrix(mat_back, 2 * block),
            conv_matrix(mat_back, 2 * block + 1),
            block_vectors(table, block),
            t_biases[block],
        )
        conv_grads[2 * block] = grad_first
        conv_grads[2 * block + 1] = grad_second
        vec_grads[block] = g_vecs
        tbias_grads[block] = jnp.sum(d_tbias, axis=0)
        d_tbias_low = d_tbias.astype(jnp.bfloat16)
        tmat_grads[block] = jnp.einsum(
            "bi,bj->ij", temb, d_tbias_low, preferred_element_type=jnp.float32
        )
        d_temb = d_temb + jnp.einsum(
            "bj,ij->bi",
            d_tbias_low,
            lin_matrix(mat_back, block),
            preferred_element_type=jnp.float32,
        )
        if block == BLOCKS - 1:
            d_skip = d_in
        d_hidden = d_in
        if block == 1:
            d_hidden = d_hidden + d_skip
    d_pre_time, g_time_bias = pull_time(d_temb)
    g_time = jnp.einsum(
        "bi,bj->ij", emb, d_pre_time.astype(jnp.bfloat16), preferred_element_type=jnp.float32
    )
    g_in_bias = jnp.sum(d_hidden, axis=(0, 1))
    g_in = jnp.einsum(
        "bfc,bfw->cw", noisy, d_hidden.astype(jnp.bfloat16), preferred_element_type=jnp.float32
    )
    vector_rows = [g_in_bias, g_time_bias, jnp.pad(g_head_bias, (0, WIDTH - FEAT))]
    for member in range(3):
        for block in range(BLOCKS):
            vector_rows = vector_rows + [vec_grads[block][member], vec_grads[block][member + 3]]
    vector_rows = vector_rows + tbias_grads
    used = 2 * FEAT + len(vector_rows)
    vec_grad = jnp.concatenate(
        [g_in, g_head, jnp.stack(vector_rows), jnp.zeros((VROWS - used, WIDTH), jnp.float32)],
        axis=0,
    )
    mat_pieces = [conv_grads[index].reshape(2 * KERNEL, half_rows, WIDTH) for index in range(OWNED)]
    mat_pieces = mat_pieces + [
        tmat_grads[block].reshape(2, half_rows, WIDTH) for block in range(BLOCKS)
    ]
    mat_grad = jnp.concatenate(mat_pieces + [g_time[None]], axis=0)
    shards = lax.axis_size("shard")
    groups = lax.axis_size("dp")
    mat_part, vec_part = (
        lax.psum_scatter(
            mat_grad.astype(jnp.bfloat16), "shard", scatter_dimension=1, tiled=True
        ).astype(jnp.float32),
        lax.psum_scatter(
            vec_grad.astype(jnp.bfloat16), "shard", scatter_dimension=0, tiled=True
        ).astype(jnp.float32),
    )
    mat_part, vec_part = lax.psum((mat_part, vec_part), "dp")
    square_local = jnp.sum(mat_part * mat_part) + jnp.sum(vec_part * vec_part)
    loss_total, square_total = lax.psum((loss_local, square_local / groups), ("dp", "shard"))
    grad_norm = jnp.sqrt(square_total) / count_total
    factor = jnp.minimum(1.0, CLIP / (grad_norm + 1e-06))
    mat_part = mat_part / count_total * factor
    vec_part = vec_part / count_total * factor
    slots = shards * soap_first.shape[0]
    choose = (owners[None, :] == jnp.arange(slots, dtype=jnp.int32)[:, None]).astype(jnp.float32)
    outgoing = jnp.einsum("sm,mrw->srw", choose, mat_part, precision=HIGH)
    incoming = lax.all_to_all(outgoing, "shard", split_axis=0, concat_axis=1, tiled=True)
    results = jax.vmap(soap_slot)(
        incoming, soap_first, soap_second, left_stat, right_stat, left_basis, right_basis
    )
    returned = lax.all_to_all(
        results[0].astype(jnp.bfloat16), "shard", split_axis=1, concat_axis=0, tiled=True
    ).astype(jnp.float32)
    update = jnp.einsum("sm,srw->mrw", choose, returned, precision=HIGH)
    new_mat = mat_weight * (1.0 - LEARN * DECAY) - LEARN * update
    new_mat_ema = EMA_RATE * mat_ema + (1.0 - EMA_RATE) * new_mat
    new_vec_first = BETA_ONE * vec_first + (1.0 - BETA_ONE) * vec_part
    new_vec_second = BETA_TWO * vec_second + (1.0 - BETA_TWO) * vec_part * vec_part
    step_vec = (
        new_vec_first
        / (1.0 - BETA_ONE**STEP)
        / (jnp.sqrt(new_vec_second / (1.0 - BETA_TWO**STEP)) + ADAM_EPS)
    )
    new_vec = vec_weight * (1.0 - TABLE_LEARN * DECAY) - TABLE_LEARN * step_vec
    new_vec_ema = EMA_RATE * vec_ema + (1.0 - EMA_RATE) * new_vec
    return (
        loss_total,
        count_total,
        grad_norm,
        new_mat,
        new_mat_ema,
        results[1],
        results[2],
        results[3],
        results[4],
        results[5],
        results[6],
        new_vec,
        new_vec_first,
        new_vec_second,
        new_vec_ema,
    )


def solution(mesh):
    placed = (
        P(("dp", "shard"), None, None),
        P(("dp", "shard"), None, None),
        P(("dp", "shard")),
        P(("dp", "shard"), None),
        P(),
        P(None, "shard", None),
        P(None, "shard", None),
        P("shard", None, None),
        P("shard", None, None),
        P("shard", None, None),
        P("shard", None, None),
        P("shard", None, None),
        P("shard", None, None),
        P("shard", None),
        P("shard", None),
        P("shard", None),
        P("shard", None),
    )
    return jax.shard_map(
        body,
        mesh=mesh,
        in_specs=placed,
        out_specs=(
            P(),
            P(),
            P(),
            P(None, "shard", None),
            P(None, "shard", None),
            P("shard", None, None),
            P("shard", None, None),
            P("shard", None, None),
            P("shard", None, None),
            P("shard", None, None),
            P("shard", None, None),
            P("shard", None),
            P("shard", None),
            P("shard", None),
            P("shard", None),
        ),
        check_vma=False,
    )
```

profile of v0, /device:TPU:1, one launch (start us, length us, event | category | flops | bytes accessed | tf_op | source)
XLA Modules:
  0.0 1083.0 jit_solution(3822976673992874667)
XLA Ops:
  9.3 23.9 %all_gather.7 = f32[128,256]{1,0:T(8,128)S(1)} all-gather(f32[8,256]{1,0:T(8,128)} %param.31), channel_id=1, replica_groups=mesh['dp'=2,'shard'=16] {'shard'}, dimensions={0}, use_global_device_ids=true | all-gather | bytes 139264 | tf_op jit(solution)/shard_map/all_gather | solution.py:222
  46.0 21.7 %all-gather.2.cloned.1.call-done = bf16[67,128,256]{2,1,0:T(8,128)(2,1)} async-done(((bf16[67,8,256]{2,1,0:T(8,128)(2,1)}), bf16[67,128,256]{2,1,0:T(8,128)(2,1)}) %all-gather.2.cloned.1.call-update) | async-done | bytes 4390928 | tf_op jit(solution)/shard_map/all_gather | solution.py:221
  67.7 4.0 fusion.295
  104.8 4.7 fusion.291
  150.2 3.6 add_reduce_fusion.1
  175.6 3.6 add_reduce_fusion
  192.1 5.2 fusion.76
  199.9 6.2 multiply_reduce_fusion
  221.1 3.7 fusion.273
  229.5 5.1 multiply_reduce_fusion.1
  251.7 3.7 fusion.274
  257.3 6.5 multiply_reduce_fusion.2
  287.8 5.1 multiply_reduce_fusion.3
  314.7 6.6 multiply_reduce_fusion.4
  345.2 5.3 multiply_reduce_fusion.5
  371.9 4.2 fusion.114
  397.3 6.5 concatenate.56
  404.0 60.8 %reduce-scatter.7.cloned.1.call-done = bf16[8,17152]{1,0:T(8,128)(2,1)} async-done(((bf16[128,17152]{1,0:T(8,128)(2,1)}), bf16[8,17152]{1,0:T(8,128)(2,1)}) %reduce-scatter.7.cloned.1.call-update) | async-done | bytes 274448
  467.4 51.2 %reduce-scatter.5.cloned.1.call-done = bf16[8,256]{1,0:T(8,128)(2,1)} async-done(((bf16[128,256]{1,0:T(8,128)(2,1)}), bf16[8,256]{1,0:T(8,128)(2,1)}) %reduce-scatter.5.cloned.1.call-update) | async-done | bytes 4112 | tf_op jit(solution)/shard_map/reduce_scatter | solution.py:328
  518.6 3.9 psum.38
  523.2 28.6 %all-reduce.20.cloned.1.call-done = f32[67,8,256]{2,1,0:T(8,128)} async-done(((f32[67,8,256]{2,1,0:T(8,128)}), f32[67,8,256]{2,1,0:T(8,128)}) %all-reduce.20.cloned.1.call-update) | async-done | bytes 548880 | tf_op jit(solution)/shard_map/psum | solution.py:332
  554.9 39.2 %all-reduce.17 = (f32[]{:T(128)}, f32[]{:T(128)}, f32[]{:T(128)}) all-reduce(f32[]{:T(128)} %get-tuple-element.168, f32[]{:T(128)S(6)} %mul_shard_map.3, f32[]{:T(128)S(6)} %div.251), channel_id=1, replica_groups=mesh['dp'=2,'shard'=16] {'dp','shard'}, use_global_device_ids=true, to_apply=%region_25.26 | all-reduce | flops 3 | bytes 24 | tf_op jit(solution)/shard_map/psum | solution.py:334
  599.2 7.1 all-to-all-start
  607.7 14.7 %all-to-all-done = f32[80,8,256]{2,1,0:T(8,128)S(1)} async-done(((f32[80,8,256]{2,1,0:T(8,128)}), f32[80,8,256]{2,1,0:T(8,128)S(1)}, u32[]{:S(2)}, u32[]{:S(2)}) %all-to-all-start) | async-done | bytes 655392 | tf_op jit(solution)/shard_map/all_to_all | solution.py:342
  635.9 60.1 %custom-call.27 = f32[5,128,128]{2,1,0:T(8,128)} custom-call(f32[5,128,128]{2,1,0:T(8,128)} %cholesky.131), custom_call_target="Cholesky" | custom-call | tf_op jit(solution)/shard_map/vmap(jit(cholesky))/cholesky | solution.py:169
  699.9 51.0 %custom-call.28 = f32[5,1,128,128]{2,3,1,0:T(8,128)} custom-call(f32[5,1,128,128]{3,2,1,0:T(8,128)} %select_bitcast_fusion), custom_call_target="InvertDiagBlocksLowerTriangular" | custom-call | tf_op jit(solution)/shard_map/vmap(jit(cholesky))/cholesky | solution.py:169
  755.6 60.1 %custom-call.29 = f32[5,128,128]{2,1,0:T(8,128)} custom-call(f32[5,128,128]{2,1,0:T(8,128)} %convolution_subtract_fusion.1), custom_call_target="Cholesky" | custom-call | tf_op jit(solution)/shard_map/vmap(jit(cholesky))/cholesky | solution.py:169
  826.4 60.1 %custom-call.25 = f32[5,128,128]{2,1,0:T(8,128)} custom-call(f32[5,128,128]{2,1,0:T(8,128)} %fusion.215), custom_call_target="Cholesky" | custom-call | tf_op jit(solution)/shard_map/vmap(jit(cholesky))/cholesky | solution.py:169
  891.4 7.7 while.1
  899.1 99.8 %custom-call.30 = f32[5,2,128,128]{2,3,1,0:T(8,128)} custom-call(f32[5,2,128,128]{3,2,1,0:T(8,128)} %bitcast.645), custom_call_target="InvertDiagBlocksLowerTriangular" | custom-call | tf_op jit(solution)/shard_map/vmap(jit(_solve_triangular))/triangular_solve | solution.py:170
  1011.7 5.5 all-to-all-start.1
  1021.1 49.1 %custom-call.26 = f32[5,1,128,128]{2,3,1,0:T(8,128)S(1)} custom-call(f32[5,1,128,128]{3,2,1,0:T(8,128)S(1)} %select_bitcast_fusion.1), custom_call_target="InvertDiagBlocksLowerTriangular" | custom-call | tf_op jit(solution)/shard_map/vmap(jit(_solve_triangular))/triangular_solve | solution.py:170
  (690 shorter events, 350.8 us)
Async XLA Ops:
  7.2 617.6 %copy-start = (f32[5,256,256]{2,1,0:T(8,128)S(1)}, f32[5,256,256]{2,1,0:T(8,128)}, u32[]{:S(2)}) copy-start(f32[5,256,256]{2,1,0:T(8,128)} %param.30) | copy-start | bytes 3932164
  7.2 28.9 %copy-start.165 = (s32[64]{0:T(128)S(1)}, s32[64]{0:T(128)}, u32[]{:S(2)}) copy-start(s32[64]{0:T(128)} %param.20) | copy-start | bytes 772
  7.2 28.9 %copy-start.68 = (f32[64,32,23]{0,1,2:T(8,128)S(1)}, f32[64,32,23]{0,1,2:T(8,128)}, u32[]{:S(2)}) copy-start(f32[64,32,23]{0,1,2:T(8,128)} %param.19) | copy-start | bytes 565252
  7.2 28.9 %copy-start.78 = (f32[64,32,23]{0,1,2:T(8,128)S(1)}, f32[64,32,23]{0,1,2:T(8,128)}, u32[]{:S(2)}) copy-start(f32[64,32,23]{0,1,2:T(8,128)} %param.18) | copy-start | bytes 565252
  7.2 29.3 %copy-start.97 = (s32[64,32]{0,1:T(8,128)S(1)}, s32[64,32]{0,1:T(8,128)}, u32[]{:S(2)}) copy-start(s32[64,32]{0,1:T(8,128)} %param.21) | copy-start | bytes 24580
  7.2 60.5 %all-gather.2.cloned.1.call-start = ((), (), s32[]{:S(2)}) async-start(), calls=%async_computation.4 | async-start | bytes 4665344 | tf_op jit(solution)/shard_map/all_gather | solution.py:221
  9.2 455.6 %reduce-scatter.7.cloned.1.call-start = ((), (), s32[]{:S(2)}) async-start(), calls=%async_computation.7 | async-start | bytes 4665344
  33.2 7.6 copy-start.94
  39.0 32.6 %copy-start.104 = (f32[1,256]{1,0:T(1,128)}, f32[1,256]{1,0:T(1,128)S(1)}, u32[]{:S(2)}) copy-start(f32[1,256]{1,0:T(1,128)S(1)} %get-tuple-element.247) | copy-start | bytes 3076
  74.7 14.3 %copy-start.1 = (f32[64,32,256]{2,1,0:T(8,128)}, f32[64,32,256]{2,1,0:T(8,128)S(1)}, u32[]{:S(2)}) copy-start(f32[64,32,256]{2,1,0:T(8,128)S(1)} %get-tuple-element.258) | copy-start | bytes 6291460
  81.9 7.1 copy-start.61
  94.2 15.3 %copy-start.7 = (f32[64,32,256]{2,1,0:T(8,128)}, f32[64,32,256]{2,1,0:T(8,128)S(1)}, u32[]{:S(2)}) copy-start(f32[64,32,256]{2,1,0:T(8,128)S(1)} %get-tuple-element.260) | copy-start | bytes 6291460
  97.6 11.8 %copy-start.57 = (f32[64,256]{1,0:T(8,128)}, f32[64,256]{1,0:T(8,128)S(1)}, u32[]{:S(2)}) copy-start(f32[64,256]{1,0:T(8,128)S(1)} %copy.500) | copy-start | bytes 196612
  113.8 15.2 %copy-start.3 = (f32[64,32,256]{2,1,0:T(8,128)}, f32[64,32,256]{2,1,0:T(8,128)S(1)}, u32[]{:S(2)}) copy-start(f32[64,32,256]{2,1,0:T(8,128)S(1)} %get-tuple-element.262) | copy-start | bytes 6291460
  117.2 11.8 %copy-start.35 = (f32[64,256]{1,0:T(8,128)}, f32[64,256]{1,0:T(8,128)S(1)}, u32[]{:S(2)}) copy-start(f32[64,256]{1,0:T(8,128)S(1)} %copy.504) | copy-start | bytes 196612
  197.3 8.8 copy-start.10
  367.9 8.2 slice-start
  367.9 9.9 slice-start.2
  391.1 127.5 %reduce-scatter.5.cloned.1.call-start = ((), (), s32[]{:S(2)}) async-start(), calls=%async_computation.6 | async-start | bytes 69632 | tf_op jit(solution)/shard_map/reduce_scatter | solution.py:328
  397.3 199.9 %copy-start.143 = (s32[67]{0:T(128)S(1)}, s32[67]{0:T(128)}, u32[]{:S(2)}) copy-start(s32[67]{0:T(128)} %param.22) | copy-start | bytes 808
  403.9 147.9 %all-reduce.20.cloned.1.call-start = ((), (), s32[]{:S(2)}) async-start(), calls=%async_computation.5 | async-start | bytes 1097728 | tf_op jit(solution)/shard_map/psum | solution.py:332
  597.2 9.1 copy-start.118
  597.2 9.1 copy-start.139
  597.3 9.1 copy-start.140
  597.3 9.1 copy-start.141
  597.3 25.1 %copy-start.69 = (f32[5,256,256]{2,1,0:T(8,128)S(1)}, f32[5,256,256]{2,1,0:T(8,128)}, u32[]{:S(2)}) copy-start(f32[5,256,256]{2,1,0:T(8,128)} %param.28) | copy-start | bytes 3932164
  599.2 23.2 %all-to-all-start = ((f32[80,8,256]{2,1,0:T(8,128)}), f32[80,8,256]{2,1,0:T(8,128)S(1)}, u32[]{:S(2)}, u32[]{:S(2)}) async-start(f32[80,8,256]{2,1,0:T(8,128)} %copy.575), calls=%async_computation.1 | async-start | bytes 1310720 | tf_op jit(solution)/shard_map/all_to_all | solution.py:342
  1009.3 7.9 copy-start.15
  1011.7 59.8 %all-to-all-start.1 = ((bf16[5,128,256]{2,0,1:T(8,128)(2,1)}), bf16[5,128,256]{2,0,1:T(8,128)(2,1)}, u32[]{:S(2)}, u32[]{:S(2)}) async-start(bf16[5,128,256]{2,0,1:T(8,128)(2,1)} %copy.583), calls=%async_computation.2 | async-start | bytes 1048576 | tf_op jit(solution)/shard_map/all_to_all | solution.py:346
  1018.4 51.9 %copy-start.20 = (f32[5,128,128]{2,1,0:T(8,128)S(1)}, f32[5,128,128]{2,1,0:T(8,128)}, u32[]{:S(2)}) copy-start(f32[5,128,128]{2,1,0:T(8,128)} %copy-done.19) | copy-start | bytes 983044
  1019.8 52.7 %copy-start.56 = (f32[67,8,256]{2,1,0:T(8,128)S(1)}, f32[67,8,256]{2,1,0:T(8,128)}, u32[]{:S(2)}) copy-start(f32[67,8,256]{2,1,0:T(8,128)} %param.23) | copy-start | bytes 1646596
  1019.8 52.7 %copy-start.75 = (f32[67,8,256]{2,1,0:T(8,128)S(1)}, f32[67,8,256]{2,1,0:T(8,128)}, u32[]{:S(2)}) copy-start(f32[67,8,256]{2,1,0:T(8,128)} %param.24) | copy-start | bytes 1646596
  (152 other events, 337.7 us)
Sparse Core Ops, SparseCore 0:
  10.8 56.8 all-gather.1
  391.2 73.5 reduce-scatter.6
  469.1 49.4 reduce-scatter.4
  521.4 30.3 all-reduce.19
where the time goes:
time: 1100 us; the launch traced here: 1080 us
  other arithmetic  549 us (50%)
  waiting for transfers between devices  177 us (16%)
  local copies, waits for them, and re-layouts  170 us (15%)
  matrix products  85.7 us (8%)
  blocking collectives  67 us (6%)
  between operations  21.4 us (2%)
  starting transfers between devices  12.7 us (1%)
    another operation x11, other arithmetic, orthonormal(): lower = jnp.linalg.cholesky(gram)  235 us
    another operation x7, other arithmetic, orthonormal(): return jax.scipy.linalg.solve_triangular(lower, matrix.T, lower=True).T  153 us
    unnamed x5, waiting for transfers between devices  60.9 us
    reduce_scatter x1, waiting for transfers between devices, body(): lax.psum_scatter(vec_grad.astype(jnp.bfloat16), 'shard', scatter_dimensio...  51.2 us
    reduce_sum x24, other arithmetic, group_norm(): spread = jnp.mean((grouped - centre) ** 2, axis=(1, 3), keepdims=True)  40.5 us
    psum x1, blocking collectives, body(): lax.psum((loss_local, square_local / groups), ('dp', 'shard'))  39.2 us
    unnamed x383, local copies, waits for them, and re-layouts  36.6 us
    reduce_sum x5, other arithmetic, group_norm(): return normed * gain + shift  28.6 us
  transfers between devices with their start and end apart: 6, of which 5 were waited for; matrix products, arithmetic and copies ran while one was open for 8% of the time, Pallas kernels for 0%

commit v1 on v0

v1 whole, which is shorter than its diff:
```python
import functools
import math

import jax
import jax.numpy as jnp
from jax import lax
from jax.experimental import pallas as pl
from jax.experimental.pallas import tpu as pltpu
from jax.sharding import PartitionSpec as P

WIDTH = 256
KERNEL = 5
GROUPS = 8
TDIM = 128
FEAT = 23
BLOCKS = 3
DSTEPS = 20
STEP = 10
OWNED = 6
UNITS = 67
VROWS = 128


HIGH = lax.Precision.HIGHEST
BETA_ONE = 0.9
BETA_TWO = 0.95
ADAM_EPS = 1e-08
LEARN = 0.05
TABLE_LEARN = 0.25
DECAY = 0.01
CLIP = 0.05
EMA_RATE = 0.8
NORM_EPS = 1e-05
PANEL = 32
LANES = 128
PAD = 8
CHUNK = 8
BASE = 2 * FEAT
F32 = jnp.float32
BF16 = jnp.bfloat16


def noise_level(steps):
    offset = 0.008
    ratio = (steps.astype(jnp.float32) + 1.0) / DSTEPS
    upper = jnp.cos((ratio + offset) / (1.0 + offset) * math.pi / 2) ** 2
    return upper / math.cos(offset / (1.0 + offset) * math.pi / 2) ** 2


def time_embed(steps):
    halfway = TDIM // 2
    freqs = jnp.exp(-math.log(10000.0) * jnp.arange(halfway, dtype=jnp.float32) / (halfway - 1))
    angles = steps.astype(jnp.float32)[:, None] * freqs[None, :]
    return jnp.concatenate([jnp.sin(angles), jnp.cos(angles)], axis=-1)


def mm(a, b, ca=1, cb=0):
    return lax.dot_general(a, b, (((ca,), (cb,)), ((), ())), precision=HIGH, preferred_element_type=jnp.float32)

def split3(v):
    hi = v.astype(jnp.bfloat16)
    rest = v - hi.astype(jnp.float32)
    mid = rest.astype(jnp.bfloat16)
    last = (rest - mid.astype(jnp.float32)).astype(jnp.bfloat16)
    return hi, mid, last

def factor_panels(chains, start):
    rows = lax.broadcasted_iota(jnp.int32, (PANEL, LANES), 0)
    lanes = lax.broadcasted_iota(jnp.int32, (PANEL, LANES), 1)
    unit = jnp.where(lanes - PANEL == rows, 1.0, 0.0).astype(jnp.float32)
    offset = lax.rem(start, LANES)
    tile = pl.multiple_of(start - offset, LANES)
    shift = lax.rem(LANES - offset, LANES)
    held = []
    for z, s, n in chains:
        block = z[s, pl.ds(start, PANEL), pl.ds(tile, LANES)]
        held.append(jnp.where(lanes < PANEL, pltpu.roll(block, shift, 1), unit))
    for k in range(PANEL):
        for c in range(len(chains)):
            e = held[c]
            column = jnp.broadcast_to(e[:, k : k + 1], (PANEL, LANES))
            pivot = column[k : k + 1, :]
            row = e[k : k + 1, :] * (1.0 / pivot)
            held[c] = e - jnp.where(rows > k, column, 0.0) * row
    for c, (z, s, n) in enumerate(chains):
        e = held[c]
        pivots = jnp.sum(jnp.where(lanes == rows, e, 0.0), axis=1, keepdims=True)
        inverse = e[:, PANEL : 2 * PANEL] * lax.rsqrt(pivots)
        panel = z[s, pl.ds(start, PANEL), :]
        done = mm(inverse, panel)
        z[s, pl.ds(start, PANEL), :] = done
        hi, mid, last = split3(done)
        lhs = jnp.concatenate([hi, hi, mid, hi, last, mid], axis=0)[:, :n]
        rhs = jnp.concatenate([hi, mid, hi, last, hi, mid], axis=0)
        for r in range(0, n, LANES):
            upd = lax.dot_general(lhs[:, r:r + LANES], rhs, (((0,), (0,)), ((), ())), preferred_element_type=jnp.float32)
            rowid = lax.broadcasted_iota(jnp.int32, (LANES, 2 * n), 0) + r
            z[s, pl.ds(r, LANES), :] = z[s, pl.ds(r, LANES), :] - jnp.where(rowid >= start + PANEL, upd, 0.0)

def soap_kernel(slots, scale, g, m, v, ls, rs, lb, rb, u_o, m_o, v_o, ls_o, rs_o, lb_o, rb_o, zl, zr):
    for s in range(slots):
        grad = g[s] * scale[0]
        left, right = lb[s], rb[s]
        first = BETA_ONE * m[s] + (1.0 - BETA_ONE) * grad
        m_o[s] = first
        turned = mm(mm(left, grad, 0, 0), right)
        second = BETA_TWO * v[s] + (1.0 - BETA_TWO) * turned * turned
        v_o[s] = second
        moment = mm(mm(left, first, 0, 0), right)
        normed = moment / (1.0 - BETA_ONE**STEP) / (jnp.sqrt(second / (1.0 - BETA_TWO**STEP)) + ADAM_EPS)
        u_o[s] = mm(mm(left, normed), right, 1, 1)
        lnew = BETA_TWO * ls[s] + (1.0 - BETA_TWO) * mm(grad, grad, 1, 1)
        rnew = BETA_TWO * rs[s] + (1.0 - BETA_TWO) * mm(grad, grad, 0, 0)
        ls_o[s] = lnew
        rs_o[s] = rnew
        xl = mm(left, lnew, 0, 1)
        xr = mm(right, rnew, 0, 1)
        zl[s, :, : LANES] = mm(xl, xl, 1, 1)
        zl[s, :, LANES:] = xl
        zr[s, :, : 2 * LANES] = mm(xr, xr, 1, 1)
        zr[s, :, 2 * LANES :] = xr
    lc = [(zl, s, LANES) for s in range(slots)]
    rc = [(zr, s, 2 * LANES) for s in range(slots)]
    def both(p, _):
        factor_panels(rc + lc, pl.multiple_of(p * PANEL, PANEL))
        return 0
    def only(p, _):
        factor_panels(rc, pl.multiple_of(p * PANEL, PANEL))
        return 0
    lax.fori_loop(0, LANES // PANEL, both, 0)
    lax.fori_loop(LANES // PANEL, 2 * LANES // PANEL, only, 0)
    for s in range(slots):
        lb_o[s] = zl[s, :, LANES:].T
        rb_o[s] = zr[s, :, 2 * LANES :].T

def soap(scale, g, m, v, ls, rs, lb, rb):
    slots = g.shape[0]
    f = jax.ShapeDtypeStruct
    vm = pl.BlockSpec(memory_space=pltpu.VMEM)
    outs = [f(x.shape, jnp.float32) for x in (g, m, v, ls, rs, lb, rb)]
    return pl.pallas_call(
        functools.partial(soap_kernel, slots),
        out_shape=outs,
        in_specs=[pl.BlockSpec(memory_space=pltpu.SMEM)] + [vm] * 7,
        out_specs=[vm] * 7,
        scratch_shapes=[pltpu.VMEM((slots, LANES, 2 * LANES), jnp.float32), pltpu.VMEM((slots, 2 * LANES, 4 * LANES), jnp.float32)],
        compiler_params=pltpu.CompilerParams(vmem_limit_bytes=56 * 2**20),
        name="soap",
    )(scale, g, m, v, ls, rs, lb, rb)


def dot(a, b, ca=1, cb=0):
    return lax.dot_general(a, b, (((ca,), (cb,)), ((), ())), preferred_element_type=F32)


def mish_parts(v):
    e = jnp.exp(jnp.minimum(v, 20.0))
    n = e * (e + 2.0)
    r = pl.reciprocal(n + 2.0)
    return e, r, n * r


def mish_slope(v, e, r, t):
    return t + v * (4.0 * e * (e + 1.0)) * (r * r)


def net_kernel(trajs, frames, emb, noisy, noise, mask, table, mats, gmat, mat_o, vec_o, loss_o,
               xin, xhat, h, skip, d, dskip, dy, u, xp, s_one, s_two, mean, rstd, xsum, q_one, q_two, g_one, g_two, tb, dtb, dpl, acc):
    rows_c = CHUNK * frames
    chunks = trajs // CHUNK
    low = table[: 2 * FEAT, :].astype(BF16)
    w_in, w_head = low[:FEAT], low[FEAT : 2 * FEAT]
    group = gmat[...]
    part = 1.0 / (frames * (WIDTH // GROUPS))

    def rows_of(c):
        return pl.ds(pl.multiple_of(c * rows_c, rows_c), rows_c)

    def trajs_of(c):
        return pl.ds(pl.multiple_of(c * CHUNK, CHUNK), CHUNK)

    def wide(v):
        return v.reshape(CHUNK, frames, WIDTH)

    def flat(v):
        return v.reshape(rows_c, WIDTH)

    def row(index):
        return table[index : index + 1, :]

    def gain(l):
        return row(BASE + 3 + OWNED + l), row(BASE + 3 + 2 * OWNED + l)

    def conv(l):
        return mats[2 * KERNEL * l : 2 * KERNEL * (l + 1)].reshape(KERNEL * WIDTH, WIDTH)

    def lin(j):
        start = 2 * KERNEL * OWNED + 2 * j
        return mats[start : start + 2].reshape(WIDTH, WIDTH)

    def group_sum(v):
        return lax.dot_general(v, group, (((1,), (0,)), ((), ())), precision=HIGH, preferred_element_type=F32)

    def spread(c, value, flip):
        for half in range(2):
            xp[half, :, PAD : PAD + frames, :] = value[:, half * LANES : (half + 1) * LANES].reshape(CHUNK, frames, LANES)
        for k in range(KERNEL):
            at = PAD + (KERNEL // 2 - k if flip else k - KERNEL // 2)
            for half in range(2):
                lane = k * WIDTH + half * LANES
                u[rows_of(c), lane : lane + LANES] = xp[half, :, at : at + frames, :].reshape(rows_c, LANES).astype(BF16)

    def pass_one(l, c, x):
        xin[l, rows_of(c), :] = x.astype(BF16)
        spread(c, x, False)
        p = dot(u[rows_of(c), :], conv(l)) + row(BASE + 3 + l)
        xhat[l, rows_of(c), :] = p
        p = wide(p)
        total = jnp.sum(p, axis=1)
        s_one[trajs_of(c), :] = total
        off = p - (total * (1.0 / frames))[:, None, :]
        s_two[trajs_of(c), :] = jnp.sum(off * off, axis=1)

    def stats(l):
        total = s_one[...]
        centre = group_sum(total) * part
        off = total * (1.0 / frames) - centre
        var = group_sum(s_two[...] + frames * off * off) * part
        scale = lax.rsqrt(var + NORM_EPS)
        mean[...] = centre
        rstd[l] = scale
        xsum[l] = frames * off * scale

    def normed(l, c):
        p = wide(xhat[l, rows_of(c), :])
        x = flat((p - mean[trajs_of(c), :][:, None, :]) * rstd[l, trajs_of(c), :][:, None, :])
        xhat[l, rows_of(c), :] = x
        g, s = gain(l)
        return x, x * g + s

    def pass_a(l, c, dm, x, v, parts):
        slope = dm * mish_slope(v, *parts)
        dy[rows_of(c), :] = slope
        q_one[trajs_of(c), :] = jnp.sum(wide(slope), axis=1)
        q_two[trajs_of(c), :] = jnp.sum(wide(slope * x), axis=1)

    def pass_a_load(l, c, dm):
        x = xhat[l, rows_of(c), :]
        g, s = gain(l)
        v = x * g + s
        pass_a(l, c, dm, x, v, mish_parts(v))

    def stats_back(l):
        g, s = gain(l)
        one, two = q_one[...], q_two[...]
        vec_o[BASE + 3 + OWNED + l : BASE + 4 + OWNED + l, :] = jnp.sum(two, axis=0, keepdims=True)
        vec_o[BASE + 3 + 2 * OWNED + l : BASE + 4 + 2 * OWNED + l, :] = jnp.sum(one, axis=0, keepdims=True)
        sums = group_sum(jnp.concatenate([one * g, two * g], axis=0)) * part
        first, second = sums[:trajs], sums[trajs:]
        g_one[...] = first
        g_two[...] = second
        dc = rstd[l] * (one * g - frames * first - xsum[l] * second)
        vec_o[BASE + 3 + l : BASE + 4 + l, :] = jnp.sum(dc, axis=0, keepdims=True)

    def loop(body):
        def step(c, carry):
            body(c)
            return carry

        lax.fori_loop(0, chunks, step, 0)

    vec_o[...] = jnp.zeros_like(vec_o)
    xp[...] = jnp.zeros_like(xp)
    acc[...] = jnp.zeros_like(acc)
    loss_o[...] = jnp.zeros_like(loss_o)
    pre_time = dot(emb[...], mats[UNITS - 1]) + row(BASE + 1)
    time_parts = mish_parts(pre_time)
    temb = (pre_time * time_parts[2]).astype(BF16)
    time_slope = mish_slope(pre_time, *time_parts)
    for j in range(BLOCKS):
        tb[j] = dot(temb, lin(j)) + row(BASE + 3 + 3 * OWNED + j)

    def enter(c):
        x = dot(noisy[rows_of(c), :], w_in) + row(BASE)
        h[rows_of(c), :] = x
        pass_one(0, c, x)

    loop(enter)
    for l in range(OWNED - 1):
        stats(l)

        def forward(c, l=l):
            _, v = normed(l, c)
            m = v * mish_parts(v)[2]
            if l % 2 == 0:
                m = flat(wide(m) + tb[l // 2, trajs_of(c), :][:, None, :])
            else:
                m = h[rows_of(c), :] + m
                if l == 1:
                    skip[rows_of(c), :] = m
                if l == 2 * BLOCKS - 3:
                    m = m + skip[rows_of(c), :]
                h[rows_of(c), :] = m
            pass_one(l + 1, c, m)

        loop(forward)
    stats(OWNED - 1)

    def turn(c):
        l = OWNED - 1
        x, v = normed(l, c)
        parts = mish_parts(v)
        top = (h[rows_of(c), :] + v * parts[2]).astype(BF16)
        xin[OWNED, rows_of(c), :] = top
        err = dot(top, w_head, 1, 1) + row(BASE + 2)[:, :FEAT] - noise[rows_of(c), :]
        weighted = mask[rows_of(c), :] * err
        loss_o[...] += jnp.sum(weighted * err, axis=0, keepdims=True)
        grad = 2.0 * weighted
        acc[0:1, :FEAT] += jnp.sum(grad, axis=0, keepdims=True)
        grad = grad.astype(BF16)
        dpl[rows_of(c), :] = grad
        dh = dot(grad, w_head)
        d[rows_of(c), :] = dh
        pass_a(l, c, dh, x, v, parts)

    loop(turn)
    vec_o[FEAT : 2 * FEAT, :] = dot(dpl[...], xin[OWNED], 0, 0)
    vec_o[BASE + 2 : BASE + 3, :] = acc[0:1, :]

    for l in reversed(range(OWNED)):
        stats_back(l)

        def backward(c, l=l):
            g, s = gain(l)
            at = trajs_of(c)
            x = wide(xhat[l, rows_of(c), :])
            dp = rstd[l, at, :][:, None, :] * (
                wide(dy[rows_of(c), :] * g) - g_one[at, :][:, None, :] - x * g_two[at, :][:, None, :]
            )
            spread(c, flat(dp), True)
            dx = None
            w = conv(l)
            for k in range(KERNEL):
                term = dot(u[rows_of(c), k * WIDTH : (k + 1) * WIDTH], w[k * WIDTH : (k + 1) * WIDTH], 1, 1)
                dx = term if dx is None else dx + term
            if l % 2 == 1:
                dtb[l // 2, at, :] = jnp.sum(wide(dx), axis=1)
                pass_a_load(l - 1, c, dx)
            else:
                dx = d[rows_of(c), :] + dx
                if l == OWNED - 2:
                    dskip[rows_of(c), :] = dx
                if l == 2:
                    dx = dx + dskip[rows_of(c), :]
                if l > 0:
                    d[rows_of(c), :] = dx
                    pass_a_load(l - 1, c, dx)
                else:
                    acc[8:16, :] += jnp.sum(dx.reshape(rows_c // 8, 8, WIDTH), axis=0)
                    xin[OWNED, rows_of(c), :] = dx.astype(BF16)

        loop(backward)
        w_grad = dot(xin[l], u[...], 0, 0)
        for k in range(KERNEL):
            for half in range(2):
                mat_o[2 * KERNEL * l + 2 * k + half] = w_grad[half * LANES : (half + 1) * LANES, k * WIDTH : (k + 1) * WIDTH].astype(mat_o.dtype)

    vec_o[BASE : BASE + 1, :] = jnp.sum(acc[8:16, :], axis=0, keepdims=True)
    vec_o[:FEAT, :] = dot(noisy[...], xin[OWNED], 0, 0)
    d_temb = None
    for j in range(BLOCKS):
        grads = dtb[j]
        vec_o[BASE + 3 + 3 * OWNED + j : BASE + 4 + 3 * OWNED + j, :] = jnp.sum(grads, axis=0, keepdims=True)
        grads = grads.astype(BF16)
        t_grad = dot(temb, grads, 0, 0)
        for half in range(2):
            mat_o[2 * KERNEL * OWNED + 2 * j + half] = t_grad[half * LANES : (half + 1) * LANES].astype(mat_o.dtype)
        term = dot(grads, lin(j), 1, 1)
        d_temb = term if d_temb is None else d_temb + term
    d_pre = d_temb * time_slope
    vec_o[BASE + 1 : BASE + 2, :] = jnp.sum(d_pre, axis=0, keepdims=True)
    mat_o[UNITS - 1] = dot(emb[...], d_pre.astype(BF16), 0, 0).astype(mat_o.dtype)


def net(emb, noisy, noise, mask, table, mats, frames):
    rows = noisy.shape[0]
    trajs = rows // frames
    lane = jnp.arange(WIDTH, dtype=jnp.int32) // (WIDTH // GROUPS)
    gmat = (lane[:, None] == lane[None, :]).astype(F32)
    vm = pl.BlockSpec(memory_space=pltpu.VMEM)
    f = jax.ShapeDtypeStruct
    big = pltpu.VMEM((rows, WIDTH), F32)
    small = pltpu.VMEM((trajs, WIDTH), F32)
    return pl.pallas_call(
        functools.partial(net_kernel, trajs, frames),
        out_shape=[f((UNITS, LANES, WIDTH), BF16), f((VROWS, WIDTH), F32), f((1, FEAT), F32)],
        in_specs=[vm] * 7,
        out_specs=[vm] * 3,
        scratch_shapes=[
            pltpu.VMEM((OWNED + 1, rows, WIDTH), BF16),
            pltpu.VMEM((OWNED, rows, WIDTH), F32),
            big, big, big, big, big,
            pltpu.VMEM((rows, KERNEL * WIDTH), BF16),
            pltpu.VMEM((2, CHUNK, frames + 2 * PAD, LANES), F32),
            small, small, small,
            pltpu.VMEM((OWNED, trajs, WIDTH), F32),
            pltpu.VMEM((OWNED, trajs, WIDTH), F32),
            small, small, small, small,
            pltpu.VMEM((BLOCKS, trajs, WIDTH), F32),
            pltpu.VMEM((BLOCKS, trajs, WIDTH), F32),
            pltpu.VMEM((rows, FEAT), BF16),
            pltpu.VMEM((16, WIDTH), F32),
        ],
        compiler_params=pltpu.CompilerParams(vmem_limit_bytes=60 * 2**20),
        name="net",
    )(emb, noisy, noise, mask, table, mats, gmat)


def body(
    trajectories,
    noise,
    timesteps,
    valid,
    owners,
    mat_weight,
    mat_ema,
    soap_first,
    soap_second,
    left_stat,
    right_stat,
    left_basis,
    right_basis,
    vec_weight,
    vec_first,
    vec_second,
    vec_ema,
):
    mask = valid.astype(jnp.float32)
    count_local = FEAT * jnp.sum(mask)
    count_total = lax.psum(count_local, ("dp", "shard"))
    mat_low = lax.all_gather(mat_weight.astype(jnp.bfloat16), "shard", axis=1, tiled=True)
    table = lax.all_gather(vec_weight, "shard", axis=0, tiled=True)
    level = noise_level(timesteps)[:, None, None]
    noisy = (jnp.sqrt(level) * trajectories + jnp.sqrt(1.0 - level) * noise).astype(jnp.bfloat16)
    emb = time_embed(timesteps).astype(jnp.bfloat16)
    frames = valid.shape[1]
    mat_grad, vec_grad, loss_parts = net(
        emb,
        noisy.reshape(-1, FEAT),
        noise.reshape(-1, FEAT),
        mask.reshape(-1, 1),
        table,
        mat_low,
        frames,
    )
    loss_local = jnp.sum(loss_parts)
    shards = lax.axis_size("shard")
    groups = lax.axis_size("dp")
    mat_part, vec_part = (
        lax.psum_scatter(
            mat_grad.astype(jnp.bfloat16), "shard", scatter_dimension=1, tiled=True
        ).astype(jnp.float32),
        lax.psum_scatter(
            vec_grad.astype(jnp.bfloat16), "shard", scatter_dimension=0, tiled=True
        ).astype(jnp.float32),
    )
    mat_part, vec_part = lax.psum((mat_part, vec_part), "dp")
    square_local = jnp.sum(mat_part * mat_part) + jnp.sum(vec_part * vec_part)
    loss_total, square_total = lax.psum((loss_local, square_local / groups), ("dp", "shard"))
    grad_norm = jnp.sqrt(square_total) / count_total
    factor = jnp.minimum(1.0, CLIP / (grad_norm + 1e-06))
    vec_part = vec_part / count_total * factor
    slots = shards * soap_first.shape[0]
    choose = (owners[None, :] == jnp.arange(slots, dtype=jnp.int32)[:, None]).astype(jnp.float32)
    outgoing = jnp.einsum("sm,mrw->srw", choose, mat_part, precision=HIGH)
    incoming = lax.all_to_all(outgoing, "shard", split_axis=0, concat_axis=1, tiled=True)
    scale = (factor / count_total).reshape(1)
    results = soap(
        scale, incoming, soap_first, soap_second, left_stat, right_stat, left_basis, right_basis
    )
    returned = lax.all_to_all(
        results[0].astype(jnp.bfloat16), "shard", split_axis=1, concat_axis=0, tiled=True
    ).astype(jnp.float32)
    update = jnp.einsum("sm,srw->mrw", choose, returned, precision=HIGH)
    new_mat = mat_weight * (1.0 - LEARN * DECAY) - LEARN * update
    new_mat_ema = EMA_RATE * mat_ema + (1.0 - EMA_RATE) * new_mat
    new_vec_first = BETA_ONE * vec_first + (1.0 - BETA_ONE) * vec_part
    new_vec_second = BETA_TWO * vec_second + (1.0 - BETA_TWO) * vec_part * vec_part
    step_vec = (
        new_vec_first
        / (1.0 - BETA_ONE**STEP)
        / (jnp.sqrt(new_vec_second / (1.0 - BETA_TWO**STEP)) + ADAM_EPS)
    )
    new_vec = vec_weight * (1.0 - TABLE_LEARN * DECAY) - TABLE_LEARN * step_vec
    new_vec_ema = EMA_RATE * vec_ema + (1.0 - EMA_RATE) * new_vec
    return (
        loss_total,
        count_total,
        grad_norm,
        new_mat,
        new_mat_ema,
        results[1],
        results[2],
        results[3],
        results[4],
        results[5],
        results[6],
        new_vec,
        new_vec_first,
        new_vec_second,
        new_vec_ema,
    )


def solution(mesh):
    placed = (
        P(("dp", "shard"), None, None),
        P(("dp", "shard"), None, None),
        P(("dp", "shard")),
        P(("dp", "shard"), None),
        P(),
        P(None, "shard", None),
        P(None, "shard", None),
        P("shard", None, None),
        P("shard", None, None),
        P("shard", None, None),
        P("shard", None, None),
        P("shard", None, None),
        P("shard", None, None),
        P("shard", None),
        P("shard", None),
        P("shard", None),
        P("shard", None),
    )
    return jax.shard_map(
        body,
        mesh=mesh,
        in_specs=placed,
        out_specs=(
            P(),
            P(),
            P(),
            P(None, "shard", None),
            P(None, "shard", None),
            P("shard", None, None),
            P("shard", None, None),
            P("shard", None, None),
            P("shard", None, None),
            P("shard", None, None),
            P("shard", None, None),
            P("shard", None),
            P("shard", None),
            P("shard", None),
            P("shard", None),
        ),
        check_vma=False,
    )
```

time: 1100 us -> 490 us (0.45); the launches traced: 1080 us -> 486 us
  other arithmetic: 549 us -> 10.8 us
  Pallas kernels: 0 us -> 158 us
  local copies, waits for them, and re-layouts: 170 us -> 16.5 us
  matrix products: 85.7 us -> 2.26 us
  waiting for transfers between devices: 177 us -> 193 us
    another operation x19 -> x1, other arithmetic: 389 us -> 0.2 us  [the longest x11 235 us: orthonormal(): lower = jnp.linalg.cholesky(gram)]
    pallas_call x0 -> x2, Pallas kernels: none -> 158 us  [the longest x1 82.2 us: soap(): pl.pallas_call(functools.partial(soap_kernel, slots), out_shape=outs, in_...]
    reduce_sum x56 -> x1, other arithmetic: 111 us -> 0.6 us  [body(): loss_local = jnp.sum(loss_parts)]
    dot_general x46 -> x0, matrix products: 72.6 us -> none  [the longest x7 16.6 us: conv_mat(): jnp.einsum('bfk,kw->bfw', taps, weight, preferred_element_type=jnp.float32)]
    reduce_sum x30 -> x0, local copies, waits for them, and re-layouts: 44.1 us -> none  [the longest x12 18.3 us: group_norm(): spread = jnp.mean((grouped - centre) ** 2, axis=(1, 3), keepdims=True)]
    mul x25 -> x0, local copies, waits for them, and re-layouts: 27.4 us -> none  [the longest x12 13.7 us: group_norm(): spread = jnp.mean((grouped - centre) ** 2, axis=(1, 3), keepdims=True)]
    unnamed x383 -> x33, local copies, waits for them, and re-layouts: 36.6 us -> 9.54 us
    convert_element_type x8 -> x4, other arithmetic: 22.2 us -> 3.26 us  [the longest x1 1.16 us: body(): results[0].astype(jnp.bfloat16)]
  transfers between devices with their start and end apart: 6 -> 6, of which waited for: 5 -> 5; matrix products, arithmetic and copies ran while one was open for 8% -> 3% of each run, Pallas kernels for 0% -> 0%
where the time goes in v1:
time: 490 us; the launch traced here: 486 us
  waiting for transfers between devices  193 us (39%)
  Pallas kernels  158 us (32%)
  blocking collectives  72.7 us (15%)
  between operations  19.4 us (4%)
  local copies, waits for them, and re-layouts  16.5 us (3%)
  starting transfers between devices  12.4 us (3%)
  other arithmetic  10.8 us (2%)
    pallas_call x1, Pallas kernels, soap(): pl.pallas_call(functools.partial(soap_kernel, slots), out_shape=outs, in_...  82.2 us
    pallas_call x1, Pallas kernels, net(): pl.pallas_call(functools.partial(net_kernel, trajs, frames), out_shape=[f...  76.1 us
    unnamed x5, waiting for transfers between devices  73.5 us
    reduce_scatter x1, waiting for transfers between devices, body(): lax.psum_scatter(vec_grad.astype(jnp.bfloat16), 'shard', scatter_dimensio...  51.9 us
    psum x1, blocking collectives, body(): lax.psum((loss_local, square_local / groups), ('dp', 'shard'))  43.3 us
    psum x1, waiting for transfers between devices, body(): mat_part, vec_part = lax.psum((mat_part, vec_part), 'dp')  30.3 us
    all_gather x1, blocking collectives, body(): table = lax.all_gather(vec_weight, 'shard', axis=0, tiled=True)  25.5 us
    all_gather x1, waiting for transfers between devices, body(): lax.all_gather(mat_weight.astype(jnp.bfloat16), 'shard', axis=1, tiled=True)  24.8 us
  transfers between devices with their start and end apart: 6, of which 5 were waited for; matrix products, arithmetic and copies ran while one was open for 3% of the time, Pallas kernels for 0%

profile of v1, /device:TPU:1, one launch (start us, length us, event | category | flops | bytes accessed | tf_op | source)
XLA Modules:
  0.0 485.7 jit_solution(15589960443491018780)
XLA Ops:
  7.3 1.8 convert_element_type.34
  9.2 0.7 convert_element_type.31
  9.8 1.8 copy.84
  11.8 1.6 copy.83
  13.6 2.1 reshape.85.mask
  15.6 25.5 %all_gather.6.table = f32[128,256]{1,0:T(8,128)} all-gather(f32[8,256]{1,0:T(8,128)S(1)} %copy-done.7), channel_id=1, replica_groups=mesh['dp'=2,'shard'=16] {'shard'}, dimensions={0}, use_global_device_ids=true | all-gather | bytes 139264 | tf_op jit(solution)/shard_map/all_gather | solution.py:442
  41.3 0.7 pad_maximum_fusion.emb
  42.0 0.8 compare_convert_fusion.gmat
  42.8 24.8 %all-gather.2.cloned.1.call-done.mats = bf16[67,128,256]{2,1,0:T(8,128)(2,1)} async-done(((bf16[67,8,256]{2,1,0:T(8,128)(2,1)}), bf16[67,128,256]{2,1,0:T(8,128)(2,1)}) %all-gather.2.cloned.1.call-update) | async-done | bytes 4390928 | tf_op jit(solution)/shard_map/all_gather | solution.py:441
  67.6 76.1 %net.1 = (bf16[67,128,256]{2,1,0:T(8,128)(2,1)}, f32[128,256]{1,0:T(8,128)}, f32[1,23]{1,0:T(1,128)}) custom-call(bf16[64,128]{1,0:T(8,128)(2,1)} %pad_maximum_fusion.emb, bf16[2048,23]{1,0:T(8,128)(2,1)} %bitcast.29, f32[2048,23]{1,0:T(8,128)} %bitcast.26, f32[2048,1]{1,0:T(8,128)} %reshape.85.mask, f32[128,256]{1,0:T(8,128)} %all_gather.6.table, ...), custom_call_target="tpu_custom_call" | custom-call | tf_op jit(solution)/shard_map/net/pallas_call | solution.py:394
  143.7 4.6 copy.101
  148.4 73.4 %reduce-scatter.7.cloned.1.call-done = bf16[8,17152]{1,0:T(8,128)(2,1)} async-done(((bf16[128,17152]{1,0:T(8,128)(2,1)}), bf16[8,17152]{1,0:T(8,128)(2,1)}) %reduce-scatter.7.cloned.1.call-update) | async-done | bytes 274448
  221.8 1.1 reshape.87
  222.9 0.9 copy_convert_fusion
  223.8 30.3 %all-reduce.3.cloned.1.call-done = f32[67,8,256]{2,1,0:T(8,128)} async-done(((f32[67,8,256]{2,1,0:T(8,128)}), f32[67,8,256]{2,1,0:T(8,128)}) %all-reduce.3.cloned.1.call-update) | async-done | bytes 548880 | tf_op jit(solution)/shard_map/psum | solution.py:467
  254.1 1.7 fusion.2
  255.8 1.2 copy.89
  257.1 6.2 %all-to-all-start = ((f32[80,8,256]{2,1,0:T(8,128)}), f32[80,8,256]{2,1,0:T(8,128)S(1)}, u32[]{:S(2)}, u32[]{:S(2)}) async-start(f32[80,8,256]{2,1,0:T(8,128)} %copy.89), calls=%async_computation.1 | async-start | bytes 1310720 | tf_op jit(solution)/shard_map/all_to_all | solution.py:476
  263.3 0.6 convert_element_type.37
  265.8 51.9 %reduce-scatter.5.cloned.1.call-done = bf16[8,256]{1,0:T(8,128)(2,1)} async-done(((bf16[128,256]{1,0:T(8,128)(2,1)}), bf16[8,256]{1,0:T(8,128)(2,1)}) %reduce-scatter.5.cloned.1.call-update) | async-done | bytes 4112 | tf_op jit(solution)/shard_map/reduce_scatter | solution.py:463
  317.7 3.9 psum.38
  322.3 0.7 multiply_reduce_fusion
  324.3 43.3 %all-reduce = (f32[]{:T(128)}, f32[]{:T(128)}, f32[]{:T(128)}) all-reduce(f32[]{:T(128)} %reduce_sum.36, f32[]{:T(128)S(6)} %mul_shard_map.3, f32[]{:T(128)S(6)} %div.77), channel_id=1, replica_groups=mesh['dp'=2,'shard'=16] {'dp','shard'}, use_global_device_ids=true, to_apply=%region_1.0 | all-reduce | flops 3 | bytes 24 | tf_op jit(solution)/shard_map/psum | solution.py:469
  369.7 0.9 copy.117
  370.6 82.2 %soap.1 = (f32[5,128,256]{2,1,0:T(8,128)}, f32[5,128,256]{2,1,0:T(8,128)}, f32[5,128,256]{2,1,0:T(8,128)}, f32[5,128,128]{2,1,0:T(8,128)}, f32[5,256,256]{2,1,0:...) custom-call(f32[1]{0:T(128)} %bitcast.3.scale, f32[5,128,256]{2,1,0:T(8,128)} %bitcast.28, f32[5,128,256]{2,1,0:T(8,128)} %m.1, ...), custom_call_target="tpu_custom_call" | custom-call | tf_op jit(solution)/shard_map/soap/pallas_call | solution.py:141
  452.9 1.2 convert_element_type.39
  454.0 1.0 copy.91
  455.0 6.0 %all-to-all-start.1 = ((bf16[5,128,256]{2,0,1:T(8,128)(2,1)}), bf16[5,128,256]{2,0,1:T(8,128)(2,1)S(1)}, u32[]{:S(2)}, u32[]{:S(2)}) async-start(bf16[5,128,256]{2,0,1:T(8,128)(2,1)} %copy.91), calls=%async_computation.2 | async-start | bytes 1048576 | tf_op jit(solution)/shard_map/all_to_all | solution.py:481
  461.1 1.3 multiply_add_fusion
  462.4 12.8 %all-to-all-done.1 = bf16[5,128,256]{2,0,1:T(8,128)(2,1)S(1)} async-done(((bf16[5,128,256]{2,0,1:T(8,128)(2,1)}), bf16[5,128,256]{2,0,1:T(8,128)(2,1)S(1)}, u32[]{:S(2)}, u32[]{:S(2)}) %all-to-all-start.1) | async-done | bytes 327712 | tf_op jit(solution)/shard_map/all_to_all | solution.py:481
  475.8 1.0 copy.96
  476.8 1.0 copy.97
  (50 shorter events, 3.2 us)
Async XLA Ops:
  7.2 4.5 copy-start.12
  7.2 2.6 copy-start.2
  7.2 4.5 copy-start.4
  7.2 60.4 %all-gather.2.cloned.1.call-start = ((), (), s32[]{:S(2)}) async-start(), calls=%async_computation.4 | async-start | bytes 4665344 | tf_op jit(solution)/shard_map/all_gather | solution.py:441
  9.1 212.7 %reduce-scatter.7.cloned.1.call-start = ((), (), s32[]{:S(2)}) async-start(), calls=%async_computation.7 | async-start | bytes 4665344
  9.8 3.6 copy-start.6
  11.7 3.9 copy-start.7
  148.3 105.8 %copy-start.11 = (s32[67]{0:T(128)S(1)}, s32[67]{0:T(128)}, u32[]{:S(2)}) copy-start(s32[67]{0:T(128)} %param.21) | copy-start | bytes 808
  148.3 105.8 %all-reduce.3.cloned.1.call-start = ((), (), s32[]{:S(2)}) async-start(), calls=%async_computation.5 | async-start | bytes 1097728 | tf_op jit(solution)/shard_map/psum | solution.py:467
  255.8 7.5 %copy-start.5 = (f32[128,256]{1,0:T(8,128)S(1)}, f32[128,256]{1,0:T(8,128)}, u32[]{:S(2)}) copy-start(f32[128,256]{1,0:T(8,128)} %get-tuple-element.27) | copy-start | bytes 393220
  255.8 9.4 %copy-start.13 = (f32[1,23]{1,0:T(1,128)S(1)}, f32[1,23]{1,0:T(1,128)}, u32[]{:S(2)}) copy-start(f32[1,23]{1,0:T(1,128)} %get-tuple-element.25) | copy-start | bytes 280
  255.8 66.4 %copy-start = (f32[67,8,256]{2,1,0:T(8,128)S(1)}, f32[67,8,256]{2,1,0:T(8,128)}, u32[]{:S(2)}) copy-start(f32[67,8,256]{2,1,0:T(8,128)} %all-reduce.3.cloned.1.call-done) | copy-start | bytes 1646596
  257.1 112.6 %all-to-all-start = ((f32[80,8,256]{2,1,0:T(8,128)}), f32[80,8,256]{2,1,0:T(8,128)S(1)}, u32[]{:S(2)}, u32[]{:S(2)}) async-start(f32[80,8,256]{2,1,0:T(8,128)} %copy.89), calls=%async_computation.1 | async-start | bytes 1310720 | tf_op jit(solution)/shard_map/all_to_all | solution.py:476
  263.3 54.5 %reduce-scatter.5.cloned.1.call-start = ((), (), s32[]{:S(2)}) async-start(), calls=%async_computation.6 | async-start | bytes 69632 | tf_op jit(solution)/shard_map/reduce_scatter | solution.py:463
  452.8 8.2 %copy-start.8 = (f32[8,256]{1,0:T(8,128)S(1)}, f32[8,256]{1,0:T(8,128)}, u32[]{:S(2)}) copy-start(f32[8,256]{1,0:T(8,128)} %param.33) | copy-start | bytes 24580
  452.8 8.2 %copy-start.9 = (f32[8,256]{1,0:T(8,128)S(1)}, f32[8,256]{1,0:T(8,128)}, u32[]{:S(2)}) copy-start(f32[8,256]{1,0:T(8,128)} %param.31) | copy-start | bytes 24580
  452.8 8.2 %copy-start.10 = (f32[8,256]{1,0:T(8,128)S(1)}, f32[8,256]{1,0:T(8,128)}, u32[]{:S(2)}) copy-start(f32[8,256]{1,0:T(8,128)} %param.32) | copy-start | bytes 24580
  454.0 21.2 %copy-start.1 = (f32[67,8,256]{2,1,0:T(8,128)S(1)}, f32[67,8,256]{2,1,0:T(8,128)}, u32[]{:S(2)}) copy-start(f32[67,8,256]{2,1,0:T(8,128)} %param.22) | copy-start | bytes 1646596
  454.0 21.2 %copy-start.3 = (f32[67,8,256]{2,1,0:T(8,128)S(1)}, f32[67,8,256]{2,1,0:T(8,128)}, u32[]{:S(2)}) copy-start(f32[67,8,256]{2,1,0:T(8,128)} %param.23) | copy-start | bytes 1646596
  455.0 20.1 %all-to-all-start.1 = ((bf16[5,128,256]{2,0,1:T(8,128)(2,1)}), bf16[5,128,256]{2,0,1:T(8,128)(2,1)S(1)}, u32[]{:S(2)}, u32[]{:S(2)}) async-start(bf16[5,128,256]{2,0,1:T(8,128)(2,1)} %copy.91), calls=%async_computation.2 | async-start | bytes 1048576 | tf_op jit(solution)/shard_map/all_to_all | solution.py:481
Sparse Core Ops, SparseCore 0:
  10.8 56.7 all-gather.1
  148.5 73.3 reduce-scatter.6
  224.8 29.2 all-reduce.2
  268.1 49.5 reduce-scatter.4
